TPU v7x, 512 devices: a whole 4x4x16 slice. The times are simulated.
512 devices in a mesh: dp: 16 (over z), expert: 32 (over y, x, core).
Axes of the slice: x: 4, y: 4, z: 16, core: 2. Of those that a mesh axis runs over, the one named last changes fastest.
Arguments:
- tokens: bfloat16 [65536, 1024], P(('dp', 'expert')), may hold values from -6 to 6
- grad_out: bfloat16 [65536, 1024], P(('dp', 'expert')), may hold values from -6 to 6
- expert_ids: int32 [65536, 2], P(('dp', 'expert')), may hold values from 0 to 31, all different within a row; in each aligned block of 128 rows (0 to 127, 128 to 255, ...) at most 16 rows name the same one
- route_probs: bfloat16 [65536, 2], P(('dp', 'expert')), may hold values from 0.19921875 to 1
- gate_up_weight: bfloat16 [1024, 32, 1536], P('dp', 'expert'), may hold values from -0.1875 to 0.1875
- down_weight: bfloat16 [32, 768, 1024], P('expert'), may hold values from -0.21875 to 0.21875
- gate_up_scale_index: int32 [8, 32, 2], P(None, 'expert'), may hold values from 0 to 15
- down_scale_index: int32 [32, 6], P('expert'), may hold values from 0 to 15
- scale_table: float32 [16], replicated, may hold values from 0.5 to 2
Outputs:
- token_grad: bfloat16 [65536, 1024], P(('dp', 'expert'))
- prob_grad: float32 [65536, 2], P(('dp', 'expert'))
- gate_up_grad: bfloat16 [1024, 32, 1536], P('dp', 'expert')
- down_grad: bfloat16 [32, 768, 1024], P('expert')
Inputs may be any that keep to these rules, and one draw needn't show every extreme that they name: `expert_ids`: each row names two different experts. The 128 rows of one device name one expert at most 16 times, and in every draw some device's rows name some expert exactly 16 times.
All inputs are finite; a program needn't handle non-finite values.
Results may differ from a plain program's by a relative error of at most 0.022.
Values may be sent and summed in bfloat16 or wider, within the bound.
No kernel may reach another device: no remote copies, remote signals or barrier semaphores. Data moves between devices by JAX's collectives and lax.ppermute only.
A program may use at most 64 MiB of HBM per device.

v0:
```python
import jax
import jax.numpy as jnp
from jax import lax
from jax.sharding import PartitionSpec as P

QBLOCK = 128


def lookup(level_index, level_table):
    onehot = (level_index[..., None] == jnp.arange(level_table.shape[0], dtype=jnp.int32)).astype(
        level_table.dtype
    )
    return jnp.sum(onehot * level_table, axis=-1)


def slot_tables(routes, experts, capacity):
    flat_routes = routes.reshape(-1)
    expert_hits = (flat_routes[:, None] == jnp.arange(experts, dtype=jnp.int32)[None, :]).astype(
        jnp.int32
    )
    before = jnp.cumsum(expert_hits, axis=0) - expert_hits
    slot_rank = jnp.sum(before * expert_hits, axis=1)
    destination = flat_routes * capacity + slot_rank
    table_hits = destination[:, None] == jnp.arange(experts * capacity, dtype=jnp.int32)[None, :]
    return table_hits.astype(jnp.float32).reshape(routes.shape[0], 2, experts * capacity)


def body(
    tokens,
    grad_out,
    expert_ids,
    route_probs,
    gate_up_weight,
    down_weight,
    gate_up_scale_index,
    down_scale_index,
    scale_table,
):
    high = lax.Precision.HIGHEST
    f32 = jnp.float32
    groups = lax.axis_size("expert")
    tok_dev = tokens.shape[0]
    model_width = tokens.shape[1]
    per_device = down_weight.shape[0]
    hidden = down_weight.shape[1]
    experts = per_device * groups
    capacity = 4 * tok_dev // experts
    slots_all = experts * capacity
    slot_hits = slot_tables(expert_ids, experts, capacity)
    either = (slot_hits[:, 0] + slot_hits[:, 1]).astype(jnp.bfloat16)
    row_shape = (groups, per_device, capacity, model_width)
    send_tokens = (
        jnp.einsum("ts,td->sd", either, tokens, preferred_element_type=f32)
        .astype(jnp.bfloat16)
        .reshape(row_shape)
    )
    send_grads = (
        jnp.einsum("ts,td->sd", either, grad_out, preferred_element_type=f32)
        .astype(jnp.bfloat16)
        .reshape(row_shape)
    )
    send_probs = (
        jnp.einsum("tks,tk->s", slot_hits, route_probs.astype(f32), precision=high)
        .astype(jnp.bfloat16)
        .reshape(row_shape[:3])
    )
    recv_tokens, recv_grads, recv_probs = (
        lax.all_to_all(send_tokens, "expert", split_axis=0, concat_axis=0, tiled=True),
        lax.all_to_all(send_grads, "expert", split_axis=0, concat_axis=0, tiled=True),
        lax.all_to_all(send_probs, "expert", split_axis=0, concat_axis=0, tiled=True),
    )
    level_rows = jnp.repeat(lookup(gate_up_scale_index, scale_table), QBLOCK, axis=0)
    full_scale = jnp.repeat(level_rows, hidden, axis=2)
    down_scale = jnp.repeat(lookup(down_scale_index, scale_table), QBLOCK, axis=1)
    down_eff = (down_weight.astype(f32) * down_scale[:, :, None]).astype(jnp.bfloat16)
    gathered = lax.all_gather(gate_up_weight, "dp", axis=0, tiled=True)
    gate_up_eff = (gathered.astype(f32) * full_scale).astype(jnp.bfloat16)
    projected = jnp.einsum("sjcd,djf->sjcf", recv_tokens, gate_up_eff, preferred_element_type=f32)
    gate_part = projected[..., :hidden]
    up_part = projected[..., hidden:]
    sigmoid_gate = jax.nn.sigmoid(gate_part)
    activated = gate_part * sigmoid_gate
    hidden_rows = (activated * up_part).astype(jnp.bfloat16)
    hidden_grad = jnp.einsum("sjcd,jfd->sjcf", recv_grads, down_eff, preferred_element_type=f32)
    probs_wide = recv_probs.astype(f32)[..., None]
    scaled_grad = probs_wide * hidden_grad
    gate_grad = scaled_grad * up_part * sigmoid_gate * (1.0 + gate_part * (1.0 - sigmoid_gate))
    up_grad = scaled_grad * activated
    joint_grad = jnp.concatenate([gate_grad, up_grad], axis=-1).astype(jnp.bfloat16)
    row_grads = jnp.einsum(
        "sjcf,djf->sjcd", joint_grad, gate_up_eff, preferred_element_type=f32
    ).astype(jnp.bfloat16)
    back_rows = lax.all_to_all(row_grads, "expert", split_axis=0, concat_axis=0, tiled=True)
    token_grad = jnp.dot(
        either, back_rows.reshape(slots_all, model_width), preferred_element_type=f32
    ).astype(jnp.bfloat16)
    expert_out = jnp.einsum("sjcf,jfd->sjcd", hidden_rows, down_eff, preferred_element_type=f32)
    back_out = lax.all_to_all(
        expert_out.astype(jnp.bfloat16), "expert", split_axis=0, concat_axis=0, tiled=True
    ).astype(expert_out.dtype)
    picked = jnp.einsum(
        "tks,sd->tkd", slot_hits, back_out.reshape(slots_all, model_width), precision=high
    )
    prob_grad = jnp.sum(picked * grad_out.astype(f32)[:, None, :], axis=-1)
    weighted = (probs_wide * hidden_rows.astype(f32)).astype(jnp.bfloat16)
    partial_sum = jnp.einsum("sjcd,sjcf->djf", recv_tokens, joint_grad, preferred_element_type=f32)
    gate_up_grad = lax.psum_scatter(
        (partial_sum * full_scale).astype(jnp.bfloat16), "dp", scatter_dimension=0, tiled=True
    )
    down_part = (
        jnp.einsum("sjcf,sjcd->jfd", weighted, recv_grads, preferred_element_type=f32)
        * down_scale[:, :, None]
    )
    down_grad = lax.psum(down_part.astype(jnp.bfloat16), "dp")
    return (token_grad, prob_grad, gate_up_grad, down_grad)


def solution(mesh):
    in_specs = (
        P(("dp", "expert"), None),
        P(("dp", "expert"), None),
        P(("dp", "expert"), None),
        P(("dp", "expert"), None),
        P("dp", "expert", None),
        P("expert", None, None),
        P(None, "expert", None),
        P("expert", None),
        P(),
    )
    out_specs = (
        P(("dp", "expert"), None),
        P(("dp", "expert"), None),
        P("dp", "expert", None),
        P("expert", None, None),
    )
    return jax.shard_map(body, mesh=mesh, in_specs=in_specs, out_specs=out_specs, check_vma=False)
```

profile of v0, /device:TPU:2, one launch (start us, length us, event | category | flops | bytes accessed | tf_op | source)
XLA Modules:
  0.0 354.2 jit_solution(2820792020950934844)
XLA Ops:
  12.5 9.4 %all-to-all-start = ((bf16[32,1,16]{2,1,0:T(2,128)(2,1)}), bf16[32,1,16]{2,1,0:T(2,128)(2,1)S(1)}, u32[]{:S(2)}, u32[]{:S(2)}) async-start(bf16[32,1,16]{2,1,0:T(2,128)(2,1)} %reshape.263), calls=%async_computation | async-start | bytes 32768 | tf_op jit(solution)/shard_map/all_to_all | solution.py:70
  23.5 4.5 %all-to-all-done = bf16[32,1,16]{2,1,0:T(2,128)(2,1)S(1)} async-done(((bf16[32,1,16]{2,1,0:T(2,128)(2,1)}), bf16[32,1,16]{2,1,0:T(2,128)(2,1)S(1)}, u32[]{:S(2)}, u32[]{:S(2)}) %all-to-all-start) | async-done | bytes 1056 | tf_op jit(solution)/shard_map/all_to_all | solution.py:70
  28.0 5.7 %all-to-all-start.2 = ((bf16[32,1,16,1024]{3,2,1,0:T(8,128)(2,1)}), bf16[32,1,16,1024]{3,2,1,0:T(8,128)(2,1)}, u32[]{:S(2)}, u32[]{:S(2)}) async-start(bf16[32,1,16,1024]{3,2,1,0:T(8,128)(2,1)} %bitcast.20), calls=%async_computation.2 | async-start | bytes 2097152 | tf_op jit(solution)/shard_map/all_to_all | solution.py:68
  36.4 54.6 %all-gather.2.cloned.1.call-done = bf16[1024,1,1536]{2,0,1:T(8,128)(2,1)} async-done(((bf16[64,1,1536]{2,0,1:T(8,128)(2,1)}), bf16[1024,1,1536]{2,0,1:T(8,128)(2,1)}) %all-gather.2.cloned.1.call-update) | async-done | bytes 3145744 | tf_op jit(solution)/shard_map/all_gather | solution.py:76
  91.0 3.2 copy.84
  94.2 7.4 %all-to-all-start.1 = ((bf16[32,1,16,1024]{3,2,1,0:T(8,128)(2,1)}), bf16[32,1,16,1024]{3,2,1,0:T(8,128)(2,1)}, u32[]{:S(2)}, u32[]{:S(2)}) async-start(bf16[32,1,16,1024]{3,2,1,0:T(8,128)(2,1)} %bitcast.158), calls=%async_computation.1 | async-start | bytes 2097152 | tf_op jit(solution)/shard_map/all_to_all | solution.py:69
  103.9 1.7 copy-done.1
  105.5 1.7 copy-done.2
  107.3 5.1 %convolution_bitcast_fusion = f32[32,1,16,1536]{3,0,2,1:T(8,128)} fusion(bf16[1024,1536,1]{0,1,2:T(8,128)(2,1)S(1)} %fusion.3, bf16[32,1,16,1024]{3,2,1,0:T(8,128)(2,1)} %all-to-all-done.2), kind=kOutput, calls=%fused_computation.4 | convolution fusion | flops 1610612736 | bytes 7340032 | tf_op jit(solution)/shard_map/sjcd,djf->sjcf/dot_general | solution.py:78
  112.3 5.5 %all-to-all-done.1 = bf16[32,1,16,1024]{3,2,1,0:T(8,128)(2,1)} async-done(((bf16[32,1,16,1024]{3,2,1,0:T(8,128)(2,1)}), bf16[32,1,16,1024]{3,2,1,0:T(8,128)(2,1)}, u32[]{:S(2)}, u32[]{:S(2)}) %all-to-all-start.1) | async-done | bytes 1048608 | tf_op jit(solution)/shard_map/all_to_all | solution.py:69
  117.8 5.3 %fusion.29 = (bf16[32,16,768]{2,0,1:T(8,128)(2,1)S(1)}, bf16[32,16,768]{2,0,1:T(8,128)(2,1)S(1)}, bf16[32,1,16,768]{3,0,2,1:T(8,128)(2,1)}) fusion(f32[32,1,16,1536]{3,0,2,1:T(8,128)} %convolution_bitcast_fusion, bf16[32,1,16,1024]{3,2,1,0:T(8,128)(2,1)} %all-to-all-done.1, bf16[1,768,1024]{2,1,0:T(8,128)(2,1)S(1)} %copy-done.11, f32[768]{0:T(1024)S(1)} %copy-done.8, ...), kind=kOutput, calls=%fused_computation.46 | convolution fusion | flops 813957120 | bytes 8131584 | tf_op jit(solution)/shard_map/sjcd,jfd->sjcf/dot_general | solution.py:84
  123.2 3.8 %fusion.15 = f32[1536,1024,1]{1,0,2:T(8,128)S(1)} fusion(bf16[32,16,768]{2,0,1:T(8,128)(2,1)S(1)} %get-tuple-element.25, bf16[32,16,768]{2,0,1:T(8,128)(2,1)S(1)} %get-tuple-element.24, bf16[32,1,16,1024]{3,2,1,0:T(8,128)(2,1)} %all-to-all-done.2), kind=kOutput, calls=%fused_computation.33 | convolution fusion | flops 1613758464 | bytes 8912896 | tf_op jit(solution)/shard_map/sjcd,sjcf->djf/dot_general | solution.py:106
  127.0 1.8 fusion.2
  128.8 3.0 copy.104
  136.0 5.7 %all-to-all-start.4 = ((bf16[32,1,16,1024]{3,2,1,0:T(8,128)(2,1)}), bf16[32,1,16,1024]{3,2,1,0:T(8,128)(2,1)}, u32[]{:S(2)}, u32[]{:S(2)}) async-start(bf16[32,1,16,1024]{3,2,1,0:T(8,128)(2,1)} %copy.94), calls=%async_computation.4 | async-start | bytes 2097152 | tf_op jit(solution)/shard_map/all_to_all | solution.py:98
  142.0 4.1 %fusion.11 = bf16[1,768,1024]{2,1,0:T(8,128)(2,1)} fusion(f32[768]{0:T(1024)S(1)} %copy-done.8, bf16[32,1,16,1024]{3,2,1,0:T(8,128)(2,1)} %all-to-all-done.1, bf16[32,1,16,768]{3,0,2,1:T(8,128)(2,1)} %get-tuple-element.26, f32[32,16]{0,1:T(8,128)S(1)} %copy.86), kind=kOutput, calls=%fused_computation.23 | convolution fusion | flops 808058880 | bytes 3412992 | tf_op jit(solution)/shard_map/sjcf,sjcd->jfd/dot_general | solution.py:111
  146.2 3.2 fusion.13
  150.9 7.1 %all-to-all-done.4 = bf16[32,1,16,1024]{3,2,1,0:T(8,128)(2,1)} async-done(((bf16[32,1,16,1024]{3,2,1,0:T(8,128)(2,1)}), bf16[32,1,16,1024]{3,2,1,0:T(8,128)(2,1)}, u32[]{:S(2)}, u32[]{:S(2)}) %all-to-all-start.4) | async-done | bytes 1048608 | tf_op jit(solution)/shard_map/all_to_all | solution.py:98
  158.0 5.0 %all-to-all-start.3 = ((bf16[32,1,16,1024]{3,2,1,0:T(8,128)(2,1)}), bf16[32,1,16,1024]{3,2,1,0:T(8,128)(2,1)S(1)}, u32[]{:S(2)}, u32[]{:S(2)}) async-start(bf16[32,1,16,1024]{3,2,1,0:T(8,128)(2,1)} %copy.93), calls=%async_computation.3 | async-start | bytes 2097152 | tf_op jit(solution)/shard_map/all_to_all | solution.py:93
  163.1 2.4 fusion.14
  165.5 13.8 %all-to-all-done.3 = bf16[32,1,16,1024]{3,2,1,0:T(8,128)(2,1)S(1)} async-done(((bf16[32,1,16,1024]{3,2,1,0:T(8,128)(2,1)}), bf16[32,1,16,1024]{3,2,1,0:T(8,128)(2,1)S(1)}, u32[]{:S(2)}, u32[]{:S(2)}) %all-to-all-start.3) | async-done | bytes 1048608 | tf_op jit(solution)/shard_map/all_to_all | solution.py:93
  180.3 22.1 %reduce-scatter.4.cloned.1.call-done = bf16[64,1536]{1,0:T(8,128)(2,1)} async-done(((bf16[1024,1536]{1,0:T(8,128)(2,1)}), bf16[64,1536]{1,0:T(8,128)(2,1)}) %reduce-scatter.4.cloned.1.call-update) | async-done | bytes 196624
  204.4 140.6 %all-reduce.2.cloned.1.call-done = bf16[1,768,1024]{2,1,0:T(8,128)(2,1)} async-done(((bf16[1,768,1024]{2,1,0:T(8,128)(2,1)}), bf16[1,768,1024]{2,1,0:T(8,128)(2,1)}) %all-reduce.2.cloned.1.call-update) | async-done | bytes 1572880 | tf_op jit(solution)/shard_map/psum | solution.py:114
  345.0 2.7 copy.132
  (79 shorter events, 20.8 us)
Async XLA Ops:
  7.2 14.9 %copy-start = (bf16[128,1024]{1,0:T(8,128)(2,1)S(1)}, bf16[128,1024]{1,0:T(8,128)(2,1)}, u32[]{:S(2)}) copy-start(bf16[128,1024]{1,0:T(8,128)(2,1)} %param.9) | copy-start | bytes 786436
  7.2 83.8 %all-gather.2.cloned.1.call-start = ((), (), s32[]{:S(2)}) async-start(), calls=%async_computation.6 | async-start | bytes 3342336 | tf_op jit(solution)/shard_map/all_gather | solution.py:76
  10.8 11.0 %copy-start.6 = (s32[128,2]{0,1:T(2,128)}, s32[128,2]{0,1:T(2,128)S(1)}, u32[]{:S(2)}) copy-start(s32[128,2]{0,1:T(2,128)S(1)} %multiply_add_fusion) | copy-start | bytes 3076
  12.5 15.6 %all-to-all-start = ((bf16[32,1,16]{2,1,0:T(2,128)(2,1)}), bf16[32,1,16]{2,1,0:T(2,128)(2,1)S(1)}, u32[]{:S(2)}, u32[]{:S(2)}) async-start(bf16[32,1,16]{2,1,0:T(2,128)(2,1)} %reshape.263), calls=%async_computation | async-start | bytes 32768 | tf_op jit(solution)/shard_map/all_to_all | solution.py:70
  22.0 11.8 %copy-start.9 = (s32[8,1,2]{0,2,1:T(2,128)S(1)}, s32[8,1,2]{0,2,1:T(2,128)}, u32[]{:S(2)}) copy-start(s32[8,1,2]{0,2,1:T(2,128)} %param.15) | copy-start | bytes 196
  22.0 11.8 %copy-start.10 = (f32[16]{0:T(128)S(1)}, f32[16]{0:T(128)}, u32[]{:S(2)}) copy-start(f32[16]{0:T(128)} %param.17) | copy-start | bytes 196
  22.0 12.0 %copy-start.13 = (s32[1,6]{1,0:T(1,128)S(1)}, s32[1,6]{1,0:T(1,128)}, u32[]{:S(2)}) copy-start(s32[1,6]{1,0:T(1,128)} %param.16) | copy-start | bytes 76
  22.0 12.9 %copy-start.4 = (bf16[128,1024]{1,0:T(8,128)(2,1)S(1)}, bf16[128,1024]{1,0:T(8,128)(2,1)}, u32[]{:S(2)}) copy-start(bf16[128,1024]{1,0:T(8,128)(2,1)} %param.10) | copy-start | bytes 786436
  28.0 66.2 %all-to-all-start.2 = ((bf16[32,1,16,1024]{3,2,1,0:T(8,128)(2,1)}), bf16[32,1,16,1024]{3,2,1,0:T(8,128)(2,1)}, u32[]{:S(2)}, u32[]{:S(2)}) async-start(bf16[32,1,16,1024]{3,2,1,0:T(8,128)(2,1)} %bitcast.20), calls=%async_computation.2 | async-start | bytes 2097152 | tf_op jit(solution)/shard_map/all_to_all | solution.py:68
  94.2 23.6 %all-to-all-start.1 = ((bf16[32,1,16,1024]{3,2,1,0:T(8,128)(2,1)}), bf16[32,1,16,1024]{3,2,1,0:T(8,128)(2,1)}, u32[]{:S(2)}, u32[]{:S(2)}) async-start(bf16[32,1,16,1024]{3,2,1,0:T(8,128)(2,1)} %bitcast.158), calls=%async_computation.1 | async-start | bytes 2097152 | tf_op jit(solution)/shard_map/all_to_all | solution.py:69
  101.7 100.8 %reduce-scatter.4.cloned.1.call-start = ((), (), s32[]{:S(2)}) async-start(), calls=%async_computation.8 | async-start | bytes 3342336
  102.7 2.9 copy-start.1
  107.3 10.6 %copy-start.8 = (f32[768]{0:T(1024)S(1)}, f32[768]{0:T(1024)}, u32[]{:S(2)}) copy-start(f32[768]{0:T(1024)} %broadcast_bitcast_fusion.1) | copy-start | bytes 9220
  107.3 10.6 %copy-start.11 = (bf16[1,768,1024]{2,1,0:T(8,128)(2,1)S(1)}, bf16[1,768,1024]{2,1,0:T(8,128)(2,1)}, u32[]{:S(2)}) copy-start(bf16[1,768,1024]{2,1,0:T(8,128)(2,1)} %param.14) | copy-start | bytes 4718596
  117.8 9.2 %slice-start = ((s8[6291456]{0:T(1024)(128)(4,1)}), s8[4194304]{0:T(1024)(128)(4,1)S(1)}, s32[]{:S(2)}) async-start(s8[6291456]{0:T(1024)(128)(4,1)} %bitcast.155), calls=%async_computation.9 | async-start | bytes 8388608
  123.1 3.8 %copy-start.15 = (bf16[32,16,768]{2,0,1:T(8,128)(2,1)}, bf16[32,16,768]{2,0,1:T(8,128)(2,1)S(1)}, u32[]{:S(2)}) copy-start(bf16[32,16,768]{2,0,1:T(8,128)(2,1)S(1)} %get-tuple-element.24) | copy-start | bytes 2359300
  123.1 3.8 %copy-start.16 = (bf16[32,16,768]{2,0,1:T(8,128)(2,1)}, bf16[32,16,768]{2,0,1:T(8,128)(2,1)S(1)}, u32[]{:S(2)}) copy-start(bf16[32,16,768]{2,0,1:T(8,128)(2,1)S(1)} %get-tuple-element.25) | copy-start | bytes 2359300
  123.1 3.9 %slice-start.1 = ((s8[6291456]{0:T(1024)(128)(4,1)}), s8[2097152]{0:T(1024)(128)(4,1)S(1)}, s32[]{:S(2)}) async-start(s8[6291456]{0:T(1024)(128)(4,1)} %bitcast.155), calls=%async_computation.10 | async-start | bytes 4194304
  136.0 22.0 %all-to-all-start.4 = ((bf16[32,1,16,1024]{3,2,1,0:T(8,128)(2,1)}), bf16[32,1,16,1024]{3,2,1,0:T(8,128)(2,1)}, u32[]{:S(2)}, u32[]{:S(2)}) async-start(bf16[32,1,16,1024]{3,2,1,0:T(8,128)(2,1)} %copy.94), calls=%async_computation.4 | async-start | bytes 2097152 | tf_op jit(solution)/shard_map/all_to_all | solution.py:98
  141.8 4.4 %copy-start.3 = (bf16[1024,1536,1]{0,1,2:T(8,128)(2,1)S(1)}, bf16[1024,1536,1]{0,1,2:T(8,128)(2,1)}, u32[]{:S(2)}) copy-start(bf16[1024,1536,1]{0,1,2:T(8,128)(2,1)} %copy-done.2) | copy-start | bytes 9437188
  141.8 203.2 %all-reduce.2.cloned.1.call-start = ((), (), s32[]{:S(2)}) async-start(), calls=%async_computation.7 | async-start | bytes 3145728 | tf_op jit(solution)/shard_map/psum | solution.py:114
  149.3 13.7 %copy-start.5 = (bf16[128,1024]{1,0:T(8,128)(2,1)S(1)}, bf16[128,1024]{1,0:T(8,128)(2,1)}, u32[]{:S(2)}) copy-start(bf16[128,1024]{1,0:T(8,128)(2,1)} %param.10) | copy-start | bytes 786436
  149.3 13.8 %copy-start.7 = (s32[128,2]{0,1:T(2,128)S(1)}, s32[128,2]{0,1:T(2,128)}, u32[]{:S(2)}) copy-start(s32[128,2]{0,1:T(2,128)} %copy-done.6) | copy-start | bytes 3076
  158.0 21.3 %all-to-all-start.3 = ((bf16[32,1,16,1024]{3,2,1,0:T(8,128)(2,1)}), bf16[32,1,16,1024]{3,2,1,0:T(8,128)(2,1)S(1)}, u32[]{:S(2)}, u32[]{:S(2)}) async-start(bf16[32,1,16,1024]{3,2,1,0:T(8,128)(2,1)} %copy.93), calls=%async_computation.3 | async-start | bytes 2097152 | tf_op jit(solution)/shard_map/all_to_all | solution.py:93
  (3 other events, 4.7 us)
Sparse Core Ops, SparseCore 0:
  10.1 80.8 all-gather.1
  131.9 70.4 reduce-scatter.3
  205.3 139.6 all-reduce.1
where the time goes:
time: 355 us; the launch traced here: 354 us
  waiting for transfers between devices  249 us (70%)
  starting transfers between devices  33.8 us (10%)
  matrix products  29.7 us (8%)
  local copies, waits for them, and re-layouts  22.7 us (6%)
  between operations  14.1 us (4%)
  other arithmetic  4.95 us (1%)
    psum x1, waiting for transfers between devices, body(): down_grad = lax.psum(down_part.astype(jnp.bfloat16), 'dp')  141 us
    all_gather x1, waiting for transfers between devices, body(): gathered = lax.all_gather(gate_up_weight, 'dp', axis=0, tiled=True)  54.6 us
    unnamed x4, waiting for transfers between devices  22.8 us
    all_to_all x1, waiting for transfers between devices, body(): lax.all_to_all(row_grads, 'expert', split_axis=0, concat_axis=0, tiled=True)  13.8 us
    unnamed x45, local copies, waits for them, and re-layouts  13.5 us
    all_to_all x1, starting transfers between devices, body(): lax.all_to_all(send_probs, 'expert', split_axis=0, concat_axis=0, tiled=T...  9.4 us
    all_to_all x1, starting transfers between devices, body(): lax.all_to_all(send_grads, 'expert', split_axis=0, concat_axis=0, tiled=T...  7.43 us
  transfers between devices with their start and end apart: 8, of which 7 were waited for; matrix products, arithmetic and copies ran while one was open for 10% of the time, Pallas kernels for 0%

commit v1 on v0

--- a/solution.py
+++ b/solution.py
@@ -111,7 +111,7 @@
         jnp.einsum("sjcf,sjcd->jfd", weighted, recv_grads, preferred_element_type=f32)
         * down_scale[:, :, None]
     )
-    down_grad = lax.psum(down_part.astype(jnp.bfloat16), "dp")
+    down_grad = jnp.sum(lax.all_gather(down_part.astype(jnp.bfloat16), "dp"), axis=0)
     return (token_grad, prob_grad, gate_up_grad, down_grad)
 
 

time: 355 us -> 500 us (1.41)
  the two profiles are of different devices: /device:TPU:2 before, /device:TPU:1 now
where the time goes in v1:
time: 500 us; the launch traced here: 499 us
  waiting for transfers between devices  376 us (75%)
  starting transfers between devices  40.7 us (8%)
  matrix products  29.3 us (6%)
  other arithmetic  19.9 us (4%)
  local copies, waits for them, and re-layouts  19 us (4%)
  between operations  14.1 us (3%)
    all_gather x1, waiting for transfers between devices, body(): lax.all_gather(down_part.astype(jnp.bfloat16), 'dp')  282 us
    all_gather x1, waiting for transfers between devices, body(): gathered = lax.all_gather(gate_up_weight, 'dp', axis=0, tiled=True)  46.3 us
    all_to_all x1, starting transfers between devices, body(): lax.all_to_all(send_grads, 'expert', split_axis=0, concat_axis=0, tiled=T...  16.3 us
    reduce_sum x1, other arithmetic, body(): jnp.sum(lax.all_gather(down_part.astype(jnp.bfloat16), 'dp'), axis=0)  14.9 us
    all_to_all x1, waiting for transfers between devices, body(): lax.all_to_all(row_grads, 'expert', split_axis=0, concat_axis=0, tiled=True)  14.9 us
    all_to_all x1, waiting for transfers between devices, body(): lax.all_to_all(expert_out.astype(jnp.bfloat16), 'expert', split_axis=0, c...  12.5 us
    all_to_all x1, starting transfers between devices, body(): lax.all_to_all(send_probs, 'expert', split_axis=0, concat_axis=0, tiled=T...  10.4 us
    unnamed x40, local copies, waits for them, and re-layouts  10.3 us
  transfers between devices with their start and end apart: 8, of which 7 were waited for; matrix products, arithmetic and copies ran while one was open for 7% of the time, Pallas kernels for 0%

profile of v1, /device:TPU:1, one launch (start us, length us, event | category | flops | bytes accessed | tf_op | source)
XLA Modules:
  0.0 499.3 jit_solution(16903885732738212160)
XLA Ops:
  12.5 10.4 %all-to-all-start = ((bf16[32,1,16]{2,1,0:T(2,128)(2,1)}), bf16[32,1,16]{2,1,0:T(2,128)(2,1)S(1)}, u32[]{:S(2)}, u32[]{:S(2)}) async-start(bf16[32,1,16]{2,1,0:T(2,128)(2,1)} %reshape.267), calls=%async_computation | async-start | bytes 32768 | tf_op jit(solution)/shard_map/all_to_all | solution.py:70
  24.5 5.3 %all-to-all-done = bf16[32,1,16]{2,1,0:T(2,128)(2,1)S(1)} async-done(((bf16[32,1,16]{2,1,0:T(2,128)(2,1)}), bf16[32,1,16]{2,1,0:T(2,128)(2,1)S(1)}, u32[]{:S(2)}, u32[]{:S(2)}) %all-to-all-start) | async-done | bytes 1056 | tf_op jit(solution)/shard_map/all_to_all | solution.py:70
  29.8 4.9 all-to-all-start.2
  36.8 46.3 %all-gather.4.cloned.1.call-done = bf16[1024,1,1536]{2,0,1:T(8,128)(2,1)} async-done(((bf16[64,1,1536]{2,0,1:T(8,128)(2,1)}), bf16[1024,1,1536]{2,0,1:T(8,128)(2,1)}) %all-gather.4.cloned.1.call-update) | async-done | bytes 3145744 | tf_op jit(solution)/shard_map/all_gather | solution.py:76
  83.0 3.2 copy.84
  86.2 16.3 %all-to-all-start.1 = ((bf16[32,1,16,1024]{3,2,1,0:T(8,128)(2,1)}), bf16[32,1,16,1024]{3,2,1,0:T(8,128)(2,1)}, u32[]{:S(2)}, u32[]{:S(2)}) async-start(bf16[32,1,16,1024]{3,2,1,0:T(8,128)(2,1)} %bitcast.157), calls=%async_computation.1 | async-start | bytes 2097152 | tf_op jit(solution)/shard_map/all_to_all | solution.py:69
  104.8 1.7 copy-done.2
  106.5 1.7 copy-done.3
  108.2 5.1 %convolution_bitcast_fusion = f32[32,1,16,1536]{3,0,2,1:T(8,128)} fusion(bf16[1024,1536,1]{0,1,2:T(8,128)(2,1)S(1)} %fusion.3, bf16[32,1,16,1024]{3,2,1,0:T(8,128)(2,1)} %all-to-all-done.2), kind=kOutput, calls=%fused_computation.4 | convolution fusion | flops 1610612736 | bytes 7340032 | tf_op jit(solution)/shard_map/sjcd,djf->sjcf/dot_general | solution.py:78
  113.3 6.5 %all-to-all-done.1 = bf16[32,1,16,1024]{3,2,1,0:T(8,128)(2,1)} async-done(((bf16[32,1,16,1024]{3,2,1,0:T(8,128)(2,1)}), bf16[32,1,16,1024]{3,2,1,0:T(8,128)(2,1)}, u32[]{:S(2)}, u32[]{:S(2)}) %all-to-all-start.1) | async-done | bytes 1048608 | tf_op jit(solution)/shard_map/all_to_all | solution.py:69
  119.8 5.3 %fusion.28 = (bf16[32,16,768]{2,0,1:T(8,128)(2,1)S(1)}, bf16[32,16,768]{2,0,1:T(8,128)(2,1)S(1)}, bf16[32,1,16,768]{3,0,2,1:T(8,128)(2,1)}) fusion(f32[32,1,16,1536]{3,0,2,1:T(8,128)} %convolution_bitcast_fusion, bf16[32,1,16,1024]{3,2,1,0:T(8,128)(2,1)} %all-to-all-done.1, bf16[1,768,1024]{2,1,0:T(8,128)(2,1)S(1)} %copy-done.9, ...), kind=kOutput, calls=%fused_computation.45 | convolution fusion | flops 813957120 | bytes 8131584 | tf_op jit(solution)/shard_map/sjcd,jfd->sjcf/dot_general | solution.py:84
  125.1 3.8 fusion.14
  129.0 1.8 fusion.2
  130.8 2.9 copy.104
  134.9 3.7 fusion.4
  141.2 4.9 all-to-all-start.4
  146.1 3.2 fusion.12
  150.9 12.5 %all-to-all-done.4 = bf16[32,1,16,1024]{3,2,1,0:T(8,128)(2,1)} async-done(((bf16[32,1,16,1024]{3,2,1,0:T(8,128)(2,1)}), bf16[32,1,16,1024]{3,2,1,0:T(8,128)(2,1)}, u32[]{:S(2)}, u32[]{:S(2)}) %all-to-all-start.4) | async-done | bytes 1048608 | tf_op jit(solution)/shard_map/all_to_all | solution.py:98
  163.4 4.0 all-to-all-start.3
  167.5 2.4 fusion.13
  169.8 14.9 %all-to-all-done.3 = bf16[32,1,16,1024]{3,2,1,0:T(8,128)(2,1)S(1)} async-done(((bf16[32,1,16,1024]{3,2,1,0:T(8,128)(2,1)}), bf16[32,1,16,1024]{3,2,1,0:T(8,128)(2,1)S(1)}, u32[]{:S(2)}, u32[]{:S(2)}) %all-to-all-start.3) | async-done | bytes 1048608 | tf_op jit(solution)/shard_map/all_to_all | solution.py:93
  185.7 8.4 %reduce-scatter.4.cloned.1.call-done = bf16[64,1536]{1,0:T(8,128)(2,1)} async-done(((bf16[1024,1536]{1,0:T(8,128)(2,1)}), bf16[64,1536]{1,0:T(8,128)(2,1)}) %reduce-scatter.4.cloned.1.call-update) | async-done | bytes 196624
  196.2 281.7 %all-gather.6.cloned.1.call-done = bf16[12288,1024]{1,0:T(8,128)(2,1)} async-done(((bf16[768,1024]{1,0:T(8,128)(2,1)}), bf16[12288,1024]{1,0:T(8,128)(2,1)}) %all-gather.6.cloned.1.call-update) | async-done | bytes 25165840 | tf_op jit(solution)/shard_map/all_gather | solution.py:114
  477.9 14.9 %reduce.4 = bf16[768,1024]{1,0:T(8,128)(2,1)} reduce(bf16[16,768,1024]{2,1,0:T(8,128)(2,1)} %bitcast.156, bf16[]{:T(256)} %constant.15.clone.1), dimensions={0}, to_apply=%region_7.8 | reduce | flops 11796480 | bytes 26738690 | tf_op jit(solution)/shard_map/reduce_sum | solution.py:114
  (75 shorter events, 19.6 us)
Async XLA Ops:
  7.2 15.9 %copy-start = (bf16[128,1024]{1,0:T(8,128)(2,1)S(1)}, bf16[128,1024]{1,0:T(8,128)(2,1)}, u32[]{:S(2)}) copy-start(bf16[128,1024]{1,0:T(8,128)(2,1)} %param.9) | copy-start | bytes 786436
  7.2 75.9 %all-gather.4.cloned.1.call-start = ((), (), s32[]{:S(2)}) async-start(), calls=%async_computation.6 | async-start | bytes 3342336 | tf_op jit(solution)/shard_map/all_gather | solution.py:76
  12.5 17.3 %all-to-all-start = ((bf16[32,1,16]{2,1,0:T(2,128)(2,1)}), bf16[32,1,16]{2,1,0:T(2,128)(2,1)S(1)}, u32[]{:S(2)}, u32[]{:S(2)}) async-start(bf16[32,1,16]{2,1,0:T(2,128)(2,1)} %reshape.267), calls=%async_computation | async-start | bytes 32768 | tf_op jit(solution)/shard_map/all_to_all | solution.py:70
  22.9 11.8 %copy-start.7 = (s32[8,1,2]{0,2,1:T(2,128)S(1)}, s32[8,1,2]{0,2,1:T(2,128)}, u32[]{:S(2)}) copy-start(s32[8,1,2]{0,2,1:T(2,128)} %param.15) | copy-start | bytes 196
  23.0 11.8 %copy-start.8 = (f32[16]{0:T(128)S(1)}, f32[16]{0:T(128)}, u32[]{:S(2)}) copy-start(f32[16]{0:T(128)} %param.17) | copy-start | bytes 196
  23.0 12.0 %copy-start.11 = (s32[1,6]{1,0:T(1,128)S(1)}, s32[1,6]{1,0:T(1,128)}, u32[]{:S(2)}) copy-start(s32[1,6]{1,0:T(1,128)} %param.16) | copy-start | bytes 76
  23.0 12.3 %copy-start.5 = (bf16[128,1024]{1,0:T(8,128)(2,1)S(1)}, bf16[128,1024]{1,0:T(8,128)(2,1)}, u32[]{:S(2)}) copy-start(bf16[128,1024]{1,0:T(8,128)(2,1)} %param.10) | copy-start | bytes 786436
  29.8 56.4 %all-to-all-start.2 = ((bf16[32,1,16,1024]{3,2,1,0:T(8,128)(2,1)}), bf16[32,1,16,1024]{3,2,1,0:T(8,128)(2,1)}, u32[]{:S(2)}, u32[]{:S(2)}) async-start(bf16[32,1,16,1024]{3,2,1,0:T(8,128)(2,1)} %bitcast.20), calls=%async_computation.2 | async-start | bytes 2097152 | tf_op jit(solution)/shard_map/all_to_all | solution.py:68
  86.2 33.6 %all-to-all-start.1 = ((bf16[32,1,16,1024]{3,2,1,0:T(8,128)(2,1)}), bf16[32,1,16,1024]{3,2,1,0:T(8,128)(2,1)}, u32[]{:S(2)}, u32[]{:S(2)}) async-start(bf16[32,1,16,1024]{3,2,1,0:T(8,128)(2,1)} %bitcast.157), calls=%async_computation.1 | async-start | bytes 2097152 | tf_op jit(solution)/shard_map/all_to_all | solution.py:69
  102.6 91.6 %reduce-scatter.4.cloned.1.call-start = ((), (), s32[]{:S(2)}) async-start(), calls=%async_computation.8 | async-start | bytes 3342336
  103.6 2.9 copy-start.2
  106.5 1.7 copy-start.3
  108.2 11.6 %copy-start.9 = (bf16[1,768,1024]{2,1,0:T(8,128)(2,1)S(1)}, bf16[1,768,1024]{2,1,0:T(8,128)(2,1)}, u32[]{:S(2)}) copy-start(bf16[1,768,1024]{2,1,0:T(8,128)(2,1)} %param.14) | copy-start | bytes 4718596
  119.8 9.2 %slice-start = ((s8[6291456]{0:T(1024)(128)(4,1)}), s8[4194304]{0:T(1024)(128)(4,1)S(1)}, s32[]{:S(2)}) async-start(s8[6291456]{0:T(1024)(128)(4,1)} %bitcast.153), calls=%async_computation.9 | async-start | bytes 8388608
  125.1 3.8 copy-start.13
  125.1 3.8 copy-start.14
  125.1 3.9 slice-start.1
  133.7 344.1 %all-gather.6.cloned.1.call-start = ((), (), s32[]{:S(2)}) async-start(), calls=%async_computation.7 | async-start | bytes 26738688 | tf_op jit(solution)/shard_map/all_gather | solution.py:114
  134.8 3.7 copy-start.10
  139.7 6.4 %copy-start.4 = (bf16[1024,1536,1]{0,1,2:T(8,128)(2,1)S(1)}, bf16[1024,1536,1]{0,1,2:T(8,128)(2,1)}, u32[]{:S(2)}) copy-start(bf16[1024,1536,1]{0,1,2:T(8,128)(2,1)} %copy-done.3) | copy-start | bytes 9437188
  141.2 22.2 %all-to-all-start.4 = ((bf16[32,1,16,1024]{3,2,1,0:T(8,128)(2,1)}), bf16[32,1,16,1024]{3,2,1,0:T(8,128)(2,1)}, u32[]{:S(2)}, u32[]{:S(2)}) async-start(bf16[32,1,16,1024]{3,2,1,0:T(8,128)(2,1)} %copy.94), calls=%async_computation.4 | async-start | bytes 2097152 | tf_op jit(solution)/shard_map/all_to_all | solution.py:98
  149.3 18.1 %copy-start.6 = (bf16[128,1024]{1,0:T(8,128)(2,1)S(1)}, bf16[128,1024]{1,0:T(8,128)(2,1)}, u32[]{:S(2)}) copy-start(bf16[128,1024]{1,0:T(8,128)(2,1)} %param.10) | copy-start | bytes 786436
  163.4 21.3 %all-to-all-start.3 = ((bf16[32,1,16,1024]{3,2,1,0:T(8,128)(2,1)}), bf16[32,1,16,1024]{3,2,1,0:T(8,128)(2,1)S(1)}, u32[]{:S(2)}, u32[]{:S(2)}) async-start(bf16[32,1,16,1024]{3,2,1,0:T(8,128)(2,1)} %copy.93), calls=%async_computation.3 | async-start | bytes 2097152 | tf_op jit(solution)/shard_map/all_to_all | solution.py:93
  477.9 14.9 %copy-start.1 = (bf16[128,1024]{1,0:T(8,128)(2,1)S(1)}, bf16[128,1024]{1,0:T(8,128)(2,1)}, u32[]{:S(2)}) copy-start(bf16[128,1024]{1,0:T(8,128)(2,1)} %param.9) | copy-start | bytes 786436
  (1 other events, 1.1 us)
Sparse Core Ops, SparseCore 0:
  10.1 72.9 all-gather.3
  133.9 60.2 reduce-scatter.3
  196.8 281.0 all-gather.5
